TPU v7x, 32 devices: a whole 2x2x4 slice. The times are simulated.
32 devices in a mesh: seq: 8 (over z, x), dp: 4 (over y, core).
Axes of the slice: x: 2, y: 2, z: 4, core: 2. Of those that a mesh axis runs over, the one named last changes fastest.
Arguments:
- queries: bfloat16 [4, 1024, 2048], P('dp', 'seq'), may hold values from -6 to 6
- keys: bfloat16 [4, 1024, 2048], P('dp', 'seq'), may hold values from -6 to 6
- values: bfloat16 [4, 1024, 2048], P('dp', 'seq'), may hold values from -6 to 6
- out_grad: bfloat16 [4, 1024, 2048], P('dp', 'seq'), may hold values from -6 to 6
- gain: float32 [2048], replicated, may hold values from 0.1 to 1.9
Outputs:
- normed_out: bfloat16 [4, 1024, 2048], P('dp', 'seq')
- query_grad: bfloat16 [4, 1024, 2048], P('dp', 'seq')
- key_grad: bfloat16 [4, 1024, 2048], P('dp', 'seq')
- value_grad: bfloat16 [4, 1024, 2048], P('dp', 'seq')
- gain_grad: float32 [2048], replicated
All inputs are finite; a program needn't handle non-finite values.
Results may differ from a plain program's by a relative error of at most 0.0085.
Values sent between devices are 32-bit elements; how exact they have to be, the bound alone decides.
A program may use at most 192 MiB of HBM per device.

v0:
```python
import math

import jax
import jax.numpy as jnp
from jax import lax
from jax.sharding import PartitionSpec as P

HEAD = 128
GROUP = 128


def prefix(part, axis, combine, identity, reverse):
    count = lax.axis_size(axis)
    place = lax.axis_index(axis)
    ahead = count - 1 - place if reverse else place
    gathered = lax.all_gather(part, axis)
    state = jnp.zeros_like(part) + jnp.asarray(identity, part.dtype)

    def one(lap, state):
        source = count - 1 - lap if reverse else lap
        return combine(state, lax.dynamic_index_in_dim(gathered, source, 0, False))

    return lax.fori_loop(0, ahead, one, state)


def add_states(first_part, second_part):
    return first_part + second_part


def split_state(state):
    state_high = state.astype(jnp.bfloat16)
    state_low = (state - state_high.astype(jnp.float32)).astype(jnp.bfloat16)
    return (state_high, state_low)


def per_device(queries, keys, values, out_grad, gain):
    feature_width = queries.shape[2]
    head_size = HEAD
    head_count = feature_width // head_size
    block_size = GROUP

    def to_blocks(array):
        return array.reshape(-1, block_size, head_count, head_size)

    query_rows = to_blocks(queries)
    key_rows = to_blocks(keys)
    value_rows = to_blocks(values)
    grad_rows = to_blocks(out_grad)
    row_index = lax.broadcasted_iota(jnp.int32, (block_size, block_size), 0)
    col_index = lax.broadcasted_iota(jnp.int32, (block_size, block_size), 1)
    causal = (row_index >= col_index).astype(jnp.float32)
    gain_rows = gain.reshape(head_count, head_size)
    key_value = jnp.einsum(
        "nshe,nshf->nhef", key_rows, value_rows, preferred_element_type=jnp.float32
    )
    device_sum = jnp.sum(key_value, axis=0)
    empty_state = jnp.zeros_like(device_sum)
    incoming = prefix(device_sum, "seq", add_states, empty_state, False)
    states = incoming[None] + (jnp.cumsum(key_value, axis=0) - key_value)
    states_high, states_low = split_state(states)
    scores = (
        jnp.einsum("nthe,nshe->nhts", query_rows, key_rows, preferred_element_type=jnp.float32)
        * causal
    )
    weights = scores.astype(jnp.bfloat16)
    attended = jnp.einsum(
        "nhts,nshe->nthe", weights, value_rows, preferred_element_type=jnp.float32
    )
    attended = attended + jnp.einsum(
        "nthe,nhef->nthf", query_rows, states_high, preferred_element_type=jnp.float32
    )
    attended = attended + jnp.einsum(
        "nthe,nhef->nthf", query_rows, states_low, preferred_element_type=jnp.float32
    )
    mean_square = jnp.mean(attended * attended, axis=-1, keepdims=True)
    inv_rms = lax.rsqrt(mean_square + 1e-05)
    normed = attended * inv_rms
    normed_out = (normed * gain_rows).astype(jnp.bfloat16)
    grad_wide = grad_rows.astype(jnp.float32)
    grad_normed = grad_wide * gain_rows
    grad_out = inv_rms * (
        grad_normed - normed * jnp.mean(grad_normed * normed, axis=-1, keepdims=True)
    )
    grad_half = grad_out.astype(jnp.bfloat16)
    gain_part = jnp.sum(normed * grad_wide, axis=(0, 1)).reshape(feature_width)
    total_tokens = queries.shape[0] * queries.shape[1] * lax.axis_size("seq") * lax.axis_size("dp")
    gain_grad = lax.psum(gain_part, ("seq", "dp")) / math.sqrt(total_tokens)
    mixed = (
        jnp.einsum("nthe,nshe->nhts", grad_half, value_rows, preferred_element_type=jnp.float32)
        * causal
    )
    mixed_half = mixed.astype(jnp.bfloat16)
    grad_query = jnp.einsum(
        "nhts,nshe->nthe", mixed_half, key_rows, preferred_element_type=jnp.float32
    )
    grad_query = grad_query + jnp.einsum(
        "nthf,nhef->nthe", grad_half, states_high, preferred_element_type=jnp.float32
    )
    grad_query = grad_query + jnp.einsum(
        "nthf,nhef->nthe", grad_half, states_low, preferred_element_type=jnp.float32
    )
    outer = jnp.einsum("nthe,nthf->nhef", query_rows, grad_half, preferred_element_type=jnp.float32)
    outer_sum = jnp.sum(outer, axis=0)
    arriving = prefix(outer_sum, "seq", add_states, empty_state, True)
    later_sum = arriving[None] + (outer_sum[None] - jnp.cumsum(outer, axis=0))
    later_high, later_low = split_state(later_sum)
    grad_key = jnp.einsum(
        "nhts,nthe->nshe", mixed_half, query_rows, preferred_element_type=jnp.float32
    )
    grad_key = grad_key + jnp.einsum(
        "nshf,nhef->nshe", value_rows, later_high, preferred_element_type=jnp.float32
    )
    grad_key = grad_key + jnp.einsum(
        "nshf,nhef->nshe", value_rows, later_low, preferred_element_type=jnp.float32
    )
    grad_value = jnp.einsum(
        "nhts,nthf->nshf", weights, grad_half, preferred_element_type=jnp.float32
    )
    grad_value = grad_value + jnp.einsum(
        "nshe,nhef->nshf", key_rows, later_high, preferred_element_type=jnp.float32
    )
    grad_value = grad_value + jnp.einsum(
        "nshe,nhef->nshf", key_rows, later_low, preferred_element_type=jnp.float32
    )
    shape_out = queries.shape
    return (
        normed_out.reshape(shape_out),
        grad_query.astype(jnp.bfloat16).reshape(shape_out),
        grad_key.astype(jnp.bfloat16).reshape(shape_out),
        grad_value.astype(jnp.bfloat16).reshape(shape_out),
        gain_grad,
    )


def solution(mesh):
    in_specs = (
        P("dp", "seq", None),
        P("dp", "seq", None),
        P("dp", "seq", None),
        P("dp", "seq", None),
        P(),
    )
    out_specs = (
        P("dp", "seq", None),
        P("dp", "seq", None),
        P("dp", "seq", None),
        P("dp", "seq", None),
        P(),
    )
    return jax.shard_map(
        per_device, mesh=mesh, in_specs=in_specs, out_specs=out_specs, check_vma=False
    )
```

profile of v0, /device:TPU:0, one launch (start us, length us, event | category | flops | bytes accessed | tf_op | source)
XLA Modules:
  0.0 313.2 jit_solution(1967142714039223897)
XLA Ops:
  12.8 2.4 copy.48
  16.5 1.5 convolution_bitcast_fusion.3
  18.0 121.3 %all-gather.5.cloned.1.call-done = f32[128,128,128]{2,1,0:T(8,128)} async-done(((f32[16,128,128]{2,1,0:T(8,128)}), f32[128,128,128]{2,1,0:T(8,128)}) %all-gather.5.cloned.1.call-update) | async-done | bytes 8388624 | tf_op jit(solution)/shard_map/all_gather | solution.py:16
  140.8 1.9 convolution_add_fusion.5
  148.7 2.0 copy.64
  150.7 1.8 fusion.5
  153.3 1.5 convolution_bitcast_fusion.2
  154.9 1.4 convolution_add_fusion.3
  157.5 49.0 %psum.7 = f32[2048]{0:T(1024)S(1)} all-reduce(f32[2048]{0:T(1024)S(1)} %bitcast.100), channel_id=1, replica_groups=mesh['seq'=8,'dp'=4] {'seq','dp'}, use_global_device_ids=true, to_apply=%region_7.8 | all-reduce | flops 2048 | bytes 16384 | tf_op jit(solution)/shard_map/psum | solution.py:87
  207.2 2.5 fusion.32
  209.7 72.9 %all-gather.7.cloned.1.call-done = f32[128,128,128]{2,1,0:T(8,128)} async-done(((f32[16,128,128]{2,1,0:T(8,128)}), f32[128,128,128]{2,1,0:T(8,128)}) %all-gather.7.cloned.1.call-update) | async-done | bytes 8388624 | tf_op jit(solution)/shard_map/all_gather | solution.py:16
  282.7 10.6 %while.23 = (s32[]{:T(128)}, f32[16,128,128]{2,1,0:T(8,128)S(1)}, s32[]{:T(128)}, f32[8,16,128,128]{3,2,1,0:T(8,128)}, s32[]{:T(128)}, /*index=5*/s32[]{:T(128)}, s32[]{:T(128)}, s32[]{:T(128)}) while((s32[]{:T(128)}, f32[16,128,128]{2,1,0:T(8,128)S(1)}, s32[]{:T(128)}, f32[8,16,128,128]{3,2,1,0:T(8,128)}, s32[]{:T(128)}, ...), condition=%wide.region_5.6_spmd, body=%wide.region_4.5_spmd.sunk | while | flops 262150 | bytes 3145871 | solution.py:23
  282.7 1.5 bitcast_add_fusion.5
  284.3 1.5 bitcast_add_fusion.5
  285.8 1.5 bitcast_add_fusion.5
  287.3 1.5 bitcast_add_fusion.5
  288.8 1.5 bitcast_add_fusion.5
  290.3 1.5 bitcast_add_fusion.5
  291.9 1.5 bitcast_add_fusion.5
  294.7 1.5 subtract_convert_fusion
  296.2 1.9 fusion.17
  299.8 2.0 copy.66
  301.9 1.9 convolution_add_fusion.1
  303.8 1.5 fusion.7
  (67 shorter events, 20.9 us)
Async XLA Ops:
  7.2 132.2 %all-gather.5.cloned.1.call-start = ((), (), s32[]{:S(2)}) async-start(), calls=%async_computation | async-start | bytes 9437184 | tf_op jit(solution)/shard_map/all_gather | solution.py:16
  8.4 131.0 %copy-start.9 = (bf16[16,8,16,128]{3,2,1,0:T(8,128)(2,1)}, bf16[16,8,16,128]{3,2,1,0:T(8,128)(2,1)S(1)}, u32[]{:S(2)}) copy-start(bf16[16,8,16,128]{3,2,1,0:T(8,128)(2,1)S(1)} %copy.76) | copy-start | bytes 1572868
  9.7 129.7 %copy-start.3 = (bf16[16,8,16,128]{3,2,1,0:T(8,128)(2,1)}, bf16[16,8,16,128]{3,2,1,0:T(8,128)(2,1)S(1)}, u32[]{:S(2)}) copy-start(bf16[16,8,16,128]{3,2,1,0:T(8,128)(2,1)S(1)} %copy.77) | copy-start | bytes 1572868
  10.2 1.4 copy-start.16
  11.6 271.0 %all-gather.7.cloned.1.call-start = ((), (), s32[]{:S(2)}) async-start(), calls=%async_computation.1 | async-start | bytes 9437184 | tf_op jit(solution)/shard_map/all_gather | solution.py:16
  12.8 129.9 %copy-start.6 = (bf16[16,8,16,128]{3,2,1,0:T(8,128)(2,1)}, bf16[16,8,16,128]{3,2,1,0:T(8,128)(2,1)S(1)}, u32[]{:S(2)}) copy-start(bf16[16,8,16,128]{3,2,1,0:T(8,128)(2,1)S(1)} %copy.75) | copy-start | bytes 1572868
  15.7 0.8 copy-start.17
  139.4 1.2 copy-start
  139.5 3.8 %copy-start.8 = (f32[1,128,2048]{1,2,0:T(8,128)S(1)}, f32[1,128,2048]{1,2,0:T(8,128)}, u32[]{:S(2)}) copy-start(f32[1,128,2048]{1,2,0:T(8,128)} %copy.48) | copy-start | bytes 3145732
  139.5 3.8 %copy-start.18 = (f32[2048]{0:T(1024)S(1)}, f32[2048]{0:T(1024)}, u32[]{:S(2)}) copy-start(f32[2048]{0:T(1024)} %param.13) | copy-start | bytes 24580
  140.8 3.3 %copy-start.13 = (bf16[16,128,128]{2,1,0:T(8,128)(2,1)}, bf16[16,128,128]{2,1,0:T(8,128)(2,1)S(1)}, u32[]{:S(2)}) copy-start(bf16[16,128,128]{2,1,0:T(8,128)(2,1)S(1)} %subtract_convert_fusion.1) | copy-start | bytes 1572868
  145.2 0.8 copy-start.1
  150.7 5.5 %copy-start.2 = (bf16[128,16,128]{0,2,1:T(8,128)(2,1)S(1)}, bf16[128,16,128]{0,2,1:T(8,128)(2,1)}, u32[]{:S(2)}) copy-start(bf16[128,16,128]{0,2,1:T(8,128)(2,1)} %copy-done.1) | copy-start | bytes 1572868
  150.7 5.5 %copy-start.14 = (bf16[16,128,128]{2,1,0:T(8,128)(2,1)S(1)}, bf16[16,128,128]{2,1,0:T(8,128)(2,1)}, u32[]{:S(2)}) copy-start(bf16[16,128,128]{2,1,0:T(8,128)(2,1)} %copy-done.13) | copy-start | bytes 1572868
  152.5 0.8 copy-start.11
  282.7 13.5 %copy-start.4 = (bf16[16,8,16,128]{3,2,1,0:T(8,128)(2,1)S(1)}, bf16[16,8,16,128]{3,2,1,0:T(8,128)(2,1)}, u32[]{:S(2)}) copy-start(bf16[16,8,16,128]{3,2,1,0:T(8,128)(2,1)} %copy-done.3) | copy-start | bytes 1572868
  293.4 5.3 %copy-start.7 = (bf16[16,8,16,128]{3,2,1,0:T(8,128)(2,1)S(1)}, bf16[16,8,16,128]{3,2,1,0:T(8,128)(2,1)}, u32[]{:S(2)}) copy-start(bf16[16,8,16,128]{3,2,1,0:T(8,128)(2,1)} %copy-done.6) | copy-start | bytes 1572868
  294.7 4.0 %copy-start.12 = (bf16[16,128,128]{2,1,0:T(8,128)(2,1)S(1)}, bf16[16,128,128]{2,1,0:T(8,128)(2,1)}, u32[]{:S(2)}) copy-start(bf16[16,128,128]{2,1,0:T(8,128)(2,1)} %copy-done.11) | copy-start | bytes 1572868
  294.7 7.2 %copy-start.5 = (f32[16,128,128]{1,2,0:T(8,128)S(1)}, f32[16,128,128]{1,2,0:T(8,128)}, u32[]{:S(2)}) copy-start(f32[16,128,128]{1,2,0:T(8,128)} %copy.57) | copy-start | bytes 3145732
  296.2 3.6 %copy-start.15 = (bf16[16,128,128]{1,2,0:T(8,128)(2,1)}, bf16[16,128,128]{1,2,0:T(8,128)(2,1)S(1)}, u32[]{:S(2)}) copy-start(bf16[16,128,128]{1,2,0:T(8,128)(2,1)S(1)} %subtract_convert_fusion) | copy-start | bytes 1572868
  298.7 5.1 %copy-start.10 = (bf16[16,8,16,128]{3,2,1,0:T(8,128)(2,1)S(1)}, bf16[16,8,16,128]{3,2,1,0:T(8,128)(2,1)}, u32[]{:S(2)}) copy-start(bf16[16,8,16,128]{3,2,1,0:T(8,128)(2,1)} %copy-done.9) | copy-start | bytes 1572868
Sparse Core Ops, SparseCore 0:
  11.7 127.6 all-gather.4
  148.8 133.7 all-gather.6
where the time goes:
time: 314 us; the launch traced here: 313 us
  waiting for transfers between devices  194 us (62%)
  blocking collectives  49 us (16%)
  matrix products  21.6 us (7%)
  local copies, waits for them, and re-layouts  19 us (6%)
  other arithmetic  14.7 us (5%)
  between operations  14.4 us (5%)
    all_gather x2, waiting for transfers between devices, prefix(): gathered = lax.all_gather(part, axis)  194 us
    psum x1, blocking collectives, per_device(): gain_grad = lax.psum(gain_part, ('seq', 'dp')) / math.sqrt(total_tokens)  49 us
    unnamed x45, local copies, waits for them, and re-layouts  13.3 us
    add x7, other arithmetic, add_states(): return first_part + second_part  10.5 us
  transfers between devices with their start and end apart: 2, of which 2 were waited for; matrix products, arithmetic and copies ran while one was open for 5% of the time, Pallas kernels for 0%

commit v1 on v0

--- a/solution.py
+++ b/solution.py
@@ -1,12 +1,20 @@
+import functools
 import math
 
 import jax
 import jax.numpy as jnp
 from jax import lax
+from jax.experimental import pallas as pl
+from jax.experimental.pallas import tpu as pltpu
 from jax.sharding import PartitionSpec as P
 
 HEAD = 128
 GROUP = 128
+LAG_FIRST = 2
+LAG_HOP = 2
+MESH = pl.DeviceIdType.MESH
+F32 = jnp.float32
+BF16 = jnp.bfloat16
 
 
 def prefix(part, axis, combine, identity, reverse):
@@ -132,6 +140,326 @@
     )
 
 
+def dot(a, b, a_dim=1, b_dim=0):
+    return lax.dot_general(a, b, (((a_dim,), (b_dim,)), ((), ())), preferred_element_type=F32)
+
+
+def flip(index, bit):
+    return index + bit * (1 - 2 * lax.rem(lax.div(index, bit), 2))
+
+
+def kernel(
+    pairs, hops, scale,
+    q_ref, k_ref, v_ref, g_ref, gain_ref,
+    out_ref, dq_ref, dk_ref, dv_ref, gg_ref,
+    f_own, f_src, f_in, fz_in, fz_out, f_give, f_take,
+    b_own, b_src, b_in, bz_in, bz_out, b_give, b_take,
+    w_all, hi_all, lo_all, go_all, gain_sum, gain_in,
+    send, recv, gain_send, gain_recv,
+):
+    half = f_own.shape[0]
+    stages = len(hops)
+    place = lax.axis_index("seq")
+    side = lax.rem(place, 2)
+    pair = lax.div(place, 2)
+    has_before = pair > 0
+    has_after = pair < pairs - 1
+    partner = {"seq": flip(place, 1)}
+    before = {"seq": place - 2}
+    after = {"seq": place + 2}
+    own_first = side * half
+    other_first = (1 - side) * half
+
+    def greet(device):
+        pl.semaphore_signal(barrier, inc=1, device_id=device, device_id_type=MESH)
+
+    def hop_device(axis, bit):
+        return {axis: flip(lax.axis_index(axis), bit)}
+
+    barrier = pltpu.get_barrier_semaphore()
+    peers = [hop for hop in hops if hop != ("seq", 2)]
+    for axis, bit in peers:
+        greet(hop_device(axis, bit))
+
+    @pl.when(has_before)
+    def _():
+        greet(before)
+
+    @pl.when(has_after)
+    def _():
+        greet(after)
+
+    def move(kind, src, dst, c, device):
+        return pltpu.make_async_remote_copy(
+            src_ref=src.at[c], dst_ref=dst.at[c],
+            send_sem=send.at[kind, c], recv_sem=recv.at[kind, c],
+            device_id=device, device_id_type=MESH,
+        )
+
+    def fx(c):
+        return move(0, f_src, f_in, c, partner)
+
+    def fz(c, device):
+        return move(1, fz_out, fz_in, c, device)
+
+    def fg(c):
+        return move(2, f_give, f_take, c, partner)
+
+    def bx(c):
+        return move(3, b_src, b_in, c, partner)
+
+    def bz(c, device):
+        return move(4, bz_out, bz_in, c, device)
+
+    def bg(c):
+        return move(5, b_give, b_take, c, partner)
+
+    def gain_move(s):
+        axis, bit = hops[s]
+        return pltpu.make_async_remote_copy(
+            src_ref=gain_sum.at[s], dst_ref=gain_in.at[s],
+            send_sem=gain_send.at[s], recv_sem=gain_recv.at[s],
+            device_id=hop_device(axis, bit), device_id_type=MESH,
+        )
+
+    def cols(h):
+        return pl.ds(pl.multiple_of(h * HEAD, HEAD), HEAD)
+
+    row = lax.broadcasted_iota(jnp.int32, (GROUP, GROUP), 0)
+    col = lax.broadcasted_iota(jnp.int32, (GROUP, GROUP), 1)
+    causal = row >= col
+
+    def key_value(h):
+        return dot(k_ref[:, cols(h)], v_ref[:, cols(h)], 0, 0)
+
+    def local_part(h):
+        w = jnp.where(causal, dot(q_ref[:, cols(h)], k_ref[:, cols(h)], 1, 1), 0.0).astype(BF16)
+        w_all[h] = w
+        return dot(w, v_ref[:, cols(h)])
+
+    def forward(h, inner, state):
+        q = q_ref[:, cols(h)]
+        hi, lo = split_state(state)
+        hi_all[h] = hi
+        lo_all[h] = lo
+        attended = inner + dot(
+            jnp.concatenate([q, q], axis=1), jnp.concatenate([hi, lo], axis=0)
+        )
+        inv = lax.rsqrt(jnp.mean(attended * attended, axis=1, keepdims=True) + 1e-05)
+        normed = attended * inv
+        gain = gain_ref[pl.ds(h, 1), :]
+        wide = g_ref[:, cols(h)].astype(F32)
+        grad_normed = wide * gain
+        go = inv * (
+            grad_normed - normed * jnp.mean(grad_normed * normed, axis=1, keepdims=True)
+        )
+        go = go.astype(BF16)
+        go_all[h] = go
+        out_ref[:, cols(h)] = (normed * gain).astype(BF16)
+        gain_sum[0, pl.ds(h, 1), :] = jnp.sum(normed * wide, axis=0, keepdims=True)
+        return dot(q, go, 0, 0)
+
+    def backward_local(h):
+        go = go_all[h]
+        mixed = jnp.where(causal, dot(go, v_ref[:, cols(h)], 1, 1), 0.0).astype(BF16)
+        dq = dot(mixed, k_ref[:, cols(h)]) + dot(
+            jnp.concatenate([go, go], axis=1),
+            jnp.concatenate([hi_all[h], lo_all[h]], axis=1), 1, 1,
+        )
+        dq_ref[:, cols(h)] = dq.astype(BF16)
+        return dot(mixed, q_ref[:, cols(h)], 0, 0), dot(w_all[h], go, 0, 0)
+
+    def backward_later(h, parts, later):
+        hi, lo = split_state(later)
+        v = v_ref[:, cols(h)]
+        k = k_ref[:, cols(h)]
+        dk = parts[0] + dot(
+            jnp.concatenate([v, v], axis=1), jnp.concatenate([hi, lo], axis=1), 1, 1
+        )
+        dv = parts[1] + dot(
+            jnp.concatenate([k, k], axis=1), jnp.concatenate([hi, lo], axis=0)
+        )
+        dk_ref[:, cols(h)] = dk.astype(BF16)
+        dv_ref[:, cols(h)] = dv.astype(BF16)
+
+    @pl.when(jnp.logical_not(has_before))
+    def _():
+        fz_in[...] = jnp.zeros_like(fz_in)
+
+    @pl.when(jnp.logical_not(has_after))
+    def _():
+        bz_in[...] = jnp.zeros_like(bz_in)
+
+    f_src[0] = key_value(other_first)
+    ends = has_before.astype(jnp.int32) + has_after.astype(jnp.int32)
+    pl.semaphore_wait(barrier, len(peers) + ends)
+
+    fx(0).start()
+    for c in range(1, half):
+        f_src[c] = key_value(other_first + c)
+        fx(c).start()
+    for c in range(half):
+        f_own[c] = key_value(own_first + c)
+
+    lag = LAG_FIRST + LAG_HOP * (pairs - 1 - pair)
+    steps = max(half + 1 + LAG_FIRST + LAG_HOP * (pairs - 1), half + stages + 1)
+
+    def step(t, carry):
+        @pl.when(t < half)
+        def _():
+            inner = local_part(own_first + t)
+            fx(t).wait_recv()
+
+            @pl.when(has_before)
+            def _():
+                fz(t, partner).wait_recv()
+
+            past, mine, theirs = fz_in[t], f_own[t], f_in[t]
+            fz_out[t] = past + (mine + theirs)
+
+            @pl.when(has_after)
+            def _():
+                fz(t, after).start()
+
+            f_give[t] = past + jnp.where(side == 0, mine, 0.0)
+            fg(t).start()
+            b_own[t] = forward(own_first + t, inner, past + jnp.where(side == 1, theirs, 0.0))
+
+        @pl.when((t >= 1) & (t < half + 1))
+        def _():
+            c = t - 1
+            inner = local_part(other_first + c)
+            fg(c).wait_recv()
+            b_src[c] = forward(other_first + c, inner, f_take[c])
+            bx(c).start()
+
+        j = t - lag
+
+        @pl.when((j >= 0) & (j < half))
+        def _():
+            bx(j).wait_recv()
+
+            @pl.when(has_after)
+            def _():
+                bz(j, partner).wait_recv()
+
+            past, mine, theirs = bz_in[j], b_own[j], b_in[j]
+            bz_out[j] = past + (mine + theirs)
+
+            @pl.when(has_before)
+            def _():
+                bz(j, before).start()
+
+            b_give[j] = past + jnp.where(side == 1, mine, 0.0)
+            bg(j).start()
+            parts = backward_local(own_first + j)
+            backward_later(own_first + j, parts, past + jnp.where(side == 0, theirs, 0.0))
+
+        @pl.when((j >= 1) & (j < half + 1))
+        def _():
+            c = j - 1
+            parts = backward_local(other_first + c)
+            bg(c).wait_recv()
+            backward_later(other_first + c, parts, b_take[c])
+
+        for s in range(stages + 1):
+
+            @pl.when(t == half + s)
+            def _(s=s):
+                if s > 0:
+                    gain_move(s - 1).wait_recv()
+                    gain_sum[s] = gain_sum[s - 1] + gain_in[s - 1]
+                if s < stages:
+                    gain_move(s).start()
+                else:
+                    gg_ref[...] = gain_sum[s] / scale
+
+        return carry
+
+    lax.fori_loop(0, steps, step, 0)
+
+    def finish(c, carry):
+        fx(c).wait_send()
+        fg(c).wait_send()
+        bx(c).wait_send()
+        bg(c).wait_send()
+
+        @pl.when(has_after)
+        def _():
+            fz(c, after).wait_send()
+
+        @pl.when(has_before)
+        def _():
+            bz(c, before).wait_send()
+
+        return carry
+
+    lax.fori_loop(0, half, finish, 0)
+    for s in range(stages):
+        gain_move(s).wait_send()
+
+
+def fused(queries, keys, values, out_grad, gain):
+    shape = queries.shape
+    rows, width = shape[1], shape[2]
+    heads = width // HEAD
+    half = heads // 2
+    count = lax.axis_size("seq")
+    spread = lax.axis_size("dp")
+    hops = []
+    for axis, size in (("seq", count), ("dp", spread)):
+        bit = 1
+        while bit < size:
+            hops.append((axis, bit))
+            bit *= 2
+    stages = len(hops)
+    scale = math.sqrt(shape[0] * rows * count * spread)
+    flat = [a.reshape(rows, width) for a in (queries, keys, values, out_grad)]
+    state = pltpu.VMEM((half, HEAD, HEAD), F32)
+    held = pltpu.VMEM((heads, HEAD, HEAD), BF16)
+    vmem = pl.BlockSpec(memory_space=pltpu.VMEM)
+    result = pl.pallas_call(
+        functools.partial(kernel, count // 2, tuple(hops), scale),
+        out_shape=[jax.ShapeDtypeStruct((rows, width), BF16)] * 4
+        + [jax.ShapeDtypeStruct((heads, HEAD), F32)],
+        in_specs=[vmem] * 5,
+        out_specs=[vmem] * 5,
+        scratch_shapes=[state] * 14
+        + [held] * 4
+        + [
+            pltpu.VMEM((stages + 1, heads, HEAD), F32),
+            pltpu.VMEM((stages, heads, HEAD), F32),
+            pltpu.SemaphoreType.DMA((6, half)),
+            pltpu.SemaphoreType.DMA((6, half)),
+            pltpu.SemaphoreType.DMA((stages,)),
+            pltpu.SemaphoreType.DMA((stages,)),
+        ],
+        compiler_params=pltpu.CompilerParams(
+            collective_id=0, has_side_effects=True, vmem_limit_bytes=40 * 1024 * 1024
+        ),
+    )(*flat, gain.reshape(heads, HEAD))
+    return tuple(a.reshape(shape) for a in result[:4]) + (result[4].reshape(width),)
+
+
+def fits(queries):
+    def power_of_two(size):
+        return size & (size - 1) == 0
+
+    heads = queries.shape[2] // HEAD
+    return (
+        queries.shape[:2] == (1, GROUP)
+        and heads % 2 == 0
+        and lax.axis_size("seq") >= 2
+        and power_of_two(lax.axis_size("seq"))
+        and power_of_two(lax.axis_size("dp"))
+    )
+
+
+def on_device(queries, keys, values, out_grad, gain):
+    run = fused if fits(queries) else per_device
+    return run(queries, keys, values, out_grad, gain)
+
+
 def solution(mesh):
     in_specs = (
         P("dp", "seq", None),
@@ -148,5 +476,5 @@
         P(),
     )
     return jax.shard_map(
-        per_device, mesh=mesh, in_specs=in_specs, out_specs=out_specs, check_vma=False
-    )
+        on_device, mesh=mesh, in_specs=in_specs, out_specs=out_specs, check_vma=False
+    )

time: 314 us -> 84.1 us (0.27)
  waiting for transfers between devices: 194 us -> 0 us
  Pallas kernels: 0 us -> 74.4 us
  blocking collectives: 49 us -> 0 us
  matrix products: 21.6 us -> 0 us
  other arithmetic: 14.7 us -> 0 us
  between operations: 14.4 us -> 0.66 us
  local copies, waits for them, and re-layouts: 19 us -> 8.63 us
    all_gather x2 -> x0, waiting for transfers between devices: 194 us -> none  [prefix(): gathered = lax.all_gather(part, axis)]
    pallas_call x0 -> x1, Pallas kernels: none -> 74.4 us  [fused(): pl.pallas_call(functools.partial(kernel, count // 2, tuple(hops), scale),...]
    psum x1 -> x0, blocking collectives: 49 us -> none  [per_device(): gain_grad = lax.psum(gain_part, ('seq', 'dp')) / math.sqrt(total_tokens)]
    dot_general x16 -> x0, matrix products: 21.6 us -> none  [the longest x1 2.54 us: per_device(): jnp.einsum('nhts,nthf->nshf', weights, grad_half, preferred_element_type=...]
    add x7 -> x0, other arithmetic: 10.5 us -> none  [add_states(): return first_part + second_part]
    unnamed x45 -> x15, local copies, waits for them, and re-layouts: 13.3 us -> 8.63 us
  transfers between devices with their start and end apart: 2 -> 0, of which waited for: 2 -> 0; matrix products, arithmetic and copies ran while one was open for 5% -> 0% of each run, Pallas kernels for 0% -> 0%
where the time goes in v1:
time: 84.1 us; the launch traced here: 83.7 us
  Pallas kernels  74.4 us (88%)
  local copies, waits for them, and re-layouts  8.63 us (10%)
    pallas_call x1, Pallas kernels, fused(): pl.pallas_call(functools.partial(kernel, count // 2, tuple(hops), scale),...  74.4 us
    unnamed x15, local copies, waits for them, and re-layouts  8.63 us

profile of v1, /device:TPU:0, one launch (start us, length us, event | category | flops | bytes accessed | tf_op | source)
XLA Modules:
  0.0 83.7 jit_solution(17599561108204685992)
XLA Ops:
  0.6 0.0 copy-start.4
  0.6 0.7 copy-done.4
  1.3 0.0 copy-start
  1.3 1.0 %copy-done = bf16[1,128,2048]{2,1,0:T(8,128)(2,1)S(1)} copy-done((bf16[1,128,2048]{2,1,0:T(8,128)(2,1)S(1)}, bf16[1,128,2048]{2,1,0:T(8,128)(2,1)}, u32[]{:S(2)}) %copy-start) | copy-done | bytes 524312
  2.4 0.0 copy-start.1
  2.4 1.0 %copy-done.1 = bf16[1,128,2048]{2,1,0:T(8,128)(2,1)S(1)} copy-done((bf16[1,128,2048]{2,1,0:T(8,128)(2,1)S(1)}, bf16[1,128,2048]{2,1,0:T(8,128)(2,1)}, u32[]{:S(2)}) %copy-start.1) | copy-done | bytes 524312
  3.4 0.0 copy-start.2
  3.4 1.0 %copy-done.2 = bf16[1,128,2048]{2,1,0:T(8,128)(2,1)S(1)} copy-done((bf16[1,128,2048]{2,1,0:T(8,128)(2,1)S(1)}, bf16[1,128,2048]{2,1,0:T(8,128)(2,1)}, u32[]{:S(2)}) %copy-start.2) | copy-done | bytes 524312
  4.5 0.0 copy-start.3
  4.5 1.0 %copy-done.3 = bf16[1,128,2048]{2,1,0:T(8,128)(2,1)S(1)} copy-done((bf16[1,128,2048]{2,1,0:T(8,128)(2,1)S(1)}, bf16[1,128,2048]{2,1,0:T(8,128)(2,1)}, u32[]{:S(2)}) %copy-start.3) | copy-done | bytes 524312
  5.5 74.4 %shard_map.92 = (bf16[128,2048]{1,0:T(8,128)(2,1)S(1)}, bf16[128,2048]{1,0:T(8,128)(2,1)S(1)}, bf16[128,2048]{1,0:T(8,128)(2,1)S(1)}, bf16[128,2048]{1,0:T(8,128)(2,1)S(1)}, f32[16,128]{1,0:T(8,128)S(1)}) custom-call(bf16[128,2048]{1,0:T(8,128)(2,1)S(1)} %bitcast.14, bf16[128,2048]{1,0:T(8,128)(2,1)S(1)} %bitcast.15, bf16[128,2048]{1,0:T(8,128)(2,1)S(1)} %bitcast.16, ...), custom_call_target="tpu_custom_call" | custom-call | tf_op jit(solution)/shard_map/pallas_call | solution.py:421
  79.9 0.8 copy.15
  80.7 0.8 copy.16
  81.5 0.8 copy.17
  82.3 0.8 copy.18
  83.1 0.6 copy.19
Async XLA Ops:
  0.6 0.7 copy-start.4
  1.3 1.0 %copy-start = (bf16[1,128,2048]{2,1,0:T(8,128)(2,1)S(1)}, bf16[1,128,2048]{2,1,0:T(8,128)(2,1)}, u32[]{:S(2)}) copy-start(bf16[1,128,2048]{2,1,0:T(8,128)(2,1)} %param.5) | copy-start | bytes 1572868
  2.4 1.0 %copy-start.1 = (bf16[1,128,2048]{2,1,0:T(8,128)(2,1)S(1)}, bf16[1,128,2048]{2,1,0:T(8,128)(2,1)}, u32[]{:S(2)}) copy-start(bf16[1,128,2048]{2,1,0:T(8,128)(2,1)} %param.6) | copy-start | bytes 1572868
  3.4 1.0 %copy-start.2 = (bf16[1,128,2048]{2,1,0:T(8,128)(2,1)S(1)}, bf16[1,128,2048]{2,1,0:T(8,128)(2,1)}, u32[]{:S(2)}) copy-start(bf16[1,128,2048]{2,1,0:T(8,128)(2,1)} %param.7) | copy-start | bytes 1572868
  4.5 1.0 %copy-start.3 = (bf16[1,128,2048]{2,1,0:T(8,128)(2,1)S(1)}, bf16[1,128,2048]{2,1,0:T(8,128)(2,1)}, u32[]{:S(2)}) copy-start(bf16[1,128,2048]{2,1,0:T(8,128)(2,1)} %param.8) | copy-start | bytes 1572868

commit v2 on v1

--- a/solution.py
+++ b/solution.py
@@ -12,6 +12,7 @@
 GROUP = 128
 LAG_FIRST = 2
 LAG_HOP = 2
+VMEM_LIMIT = 56 * 1024 * 1024
 MESH = pl.DeviceIdType.MESH
 F32 = jnp.float32
 BF16 = jnp.bfloat16
@@ -150,12 +151,14 @@
 
 def kernel(
     pairs, hops, scale,
+    q_hbm, k_hbm, v_hbm, g_hbm, gain_hbm,
+    out_hbm, dq_hbm, dk_hbm, dv_hbm, gg_hbm,
+    f_own, f_src, f_in, fz_in, fz_out, f_give, f_take,
+    b_own, b_src, b_in, bz_in, bz_out, b_give, b_take,
+    w_all, hi_all, lo_all, go_all, inner_all, dk_all, dv_all, gain_sum, gain_in,
     q_ref, k_ref, v_ref, g_ref, gain_ref,
     out_ref, dq_ref, dk_ref, dv_ref, gg_ref,
-    f_own, f_src, f_in, fz_in, fz_out, f_give, f_take,
-    b_own, b_src, b_in, bz_in, bz_out, b_give, b_take,
-    w_all, hi_all, lo_all, go_all, gain_sum, gain_in,
-    send, recv, gain_send, gain_recv,
+    send, recv, gain_send, gain_recv, load_sem, store_sem,
 ):
     half = f_own.shape[0]
     stages = len(hops)
@@ -170,6 +173,23 @@
     own_first = side * half
     other_first = (1 - side) * half
 
+    loads = [
+        pltpu.make_async_copy(src, dst, load_sem.at[i])
+        for i, (src, dst) in enumerate((
+            (k_hbm, k_ref), (v_hbm, v_ref), (q_hbm, q_ref), (g_hbm, g_ref), (gain_hbm, gain_ref),
+        ))
+    ]
+    for load in loads:
+        load.start()
+
+    stores = [
+        pltpu.make_async_copy(src, dst, store_sem.at[i])
+        for i, (src, dst) in enumerate((
+            (out_ref, out_hbm), (dq_ref, dq_hbm), (dk_ref, dk_hbm), (dv_ref, dv_hbm),
+            (gg_ref, gg_hbm),
+        ))
+    ]
+
     def greet(device):
         pl.semaphore_signal(barrier, inc=1, device_id=device, device_id_type=MESH)
 
@@ -232,17 +252,14 @@
     def key_value(h):
         return dot(k_ref[:, cols(h)], v_ref[:, cols(h)], 0, 0)
 
-    def local_part(h):
+    def local_forward(h):
         w = jnp.where(causal, dot(q_ref[:, cols(h)], k_ref[:, cols(h)], 1, 1), 0.0).astype(BF16)
-        w_all[h] = w
-        return dot(w, v_ref[:, cols(h)])
-
-    def forward(h, inner, state):
+        return w, dot(w, v_ref[:, cols(h)])
+
+    def forward(h, state):
         q = q_ref[:, cols(h)]
         hi, lo = split_state(state)
-        hi_all[h] = hi
-        lo_all[h] = lo
-        attended = inner + dot(
+        attended = inner_all[h] + dot(
             jnp.concatenate([q, q], axis=1), jnp.concatenate([hi, lo], axis=0)
         )
         inv = lax.rsqrt(jnp.mean(attended * attended, axis=1, keepdims=True) + 1e-05)
@@ -254,33 +271,44 @@
             grad_normed - normed * jnp.mean(grad_normed * normed, axis=1, keepdims=True)
         )
         go = go.astype(BF16)
+        normed_out = (normed * gain).astype(BF16)
+        gain_part = jnp.sum(normed * wide, axis=0, keepdims=True)
+        return dot(q, go, 0, 0), hi, lo, go, normed_out, gain_part
+
+    def keep_forward(h, results):
+        outer, hi, lo, go, normed_out, gain_part = results
+        hi_all[h] = hi
+        lo_all[h] = lo
         go_all[h] = go
-        out_ref[:, cols(h)] = (normed * gain).astype(BF16)
-        gain_sum[0, pl.ds(h, 1), :] = jnp.sum(normed * wide, axis=0, keepdims=True)
-        return dot(q, go, 0, 0)
-
-    def backward_local(h):
+        out_ref[:, cols(h)] = normed_out
+        gain_sum[0, pl.ds(h, 1), :] = gain_part
+
+    def local_backward(h):
         go = go_all[h]
         mixed = jnp.where(causal, dot(go, v_ref[:, cols(h)], 1, 1), 0.0).astype(BF16)
         dq = dot(mixed, k_ref[:, cols(h)]) + dot(
             jnp.concatenate([go, go], axis=1),
             jnp.concatenate([hi_all[h], lo_all[h]], axis=1), 1, 1,
         )
-        dq_ref[:, cols(h)] = dq.astype(BF16)
-        return dot(mixed, q_ref[:, cols(h)], 0, 0), dot(w_all[h], go, 0, 0)
-
-    def backward_later(h, parts, later):
+        return dq.astype(BF16), dot(mixed, q_ref[:, cols(h)], 0, 0), dot(w_all[h], go, 0, 0)
+
+    def keep_local_backward(h, results):
+        dq_ref[:, cols(h)], dk_all[h], dv_all[h] = results
+
+    def backward(h, later):
         hi, lo = split_state(later)
         v = v_ref[:, cols(h)]
         k = k_ref[:, cols(h)]
-        dk = parts[0] + dot(
+        dk = dk_all[h] + dot(
             jnp.concatenate([v, v], axis=1), jnp.concatenate([hi, lo], axis=1), 1, 1
         )
-        dv = parts[1] + dot(
+        dv = dv_all[h] + dot(
             jnp.concatenate([k, k], axis=1), jnp.concatenate([hi, lo], axis=0)
         )
-        dk_ref[:, cols(h)] = dk.astype(BF16)
-        dv_ref[:, cols(h)] = dv.astype(BF16)
+        return dk.astype(BF16), dv.astype(BF16)
+
+    def keep_backward(h, results):
+        dk_ref[:, cols(h)], dv_ref[:, cols(h)] = results
 
     @pl.when(jnp.logical_not(has_before))
     def _():
@@ -290,16 +318,19 @@
     def _():
         bz_in[...] = jnp.zeros_like(bz_in)
 
+    loads[0].wait()
+    loads[1].wait()
     f_src[0] = key_value(other_first)
     ends = has_before.astype(jnp.int32) + has_after.astype(jnp.int32)
     pl.semaphore_wait(barrier, len(peers) + ends)
-
     fx(0).start()
     for c in range(1, half):
         f_src[c] = key_value(other_first + c)
         fx(c).start()
     for c in range(half):
         f_own[c] = key_value(own_first + c)
+    for load in loads[2:]:
+        load.wait()
 
     lag = LAG_FIRST + LAG_HOP * (pairs - 1 - pair)
     steps = max(half + 1 + LAG_FIRST + LAG_HOP * (pairs - 1), half + stages + 1)
@@ -307,7 +338,6 @@
     def step(t, carry):
         @pl.when(t < half)
         def _():
-            inner = local_part(own_first + t)
             fx(t).wait_recv()
 
             @pl.when(has_before)
@@ -323,15 +353,19 @@
 
             f_give[t] = past + jnp.where(side == 0, mine, 0.0)
             fg(t).start()
-            b_own[t] = forward(own_first + t, inner, past + jnp.where(side == 1, theirs, 0.0))
+            f_own[t] = past + jnp.where(side == 1, theirs, 0.0)
 
         @pl.when((t >= 1) & (t < half + 1))
         def _():
             c = t - 1
-            inner = local_part(other_first + c)
             fg(c).wait_recv()
-            b_src[c] = forward(other_first + c, inner, f_take[c])
+            theirs = forward(other_first + c, f_take[c])
+            mine = forward(own_first + c, f_own[c])
+            b_src[c] = theirs[0]
             bx(c).start()
+            b_own[c] = mine[0]
+            keep_forward(other_first + c, theirs)
+            keep_forward(own_first + c, mine)
 
         j = t - lag
 
@@ -352,15 +386,31 @@
 
             b_give[j] = past + jnp.where(side == 1, mine, 0.0)
             bg(j).start()
-            parts = backward_local(own_first + j)
-            backward_later(own_first + j, parts, past + jnp.where(side == 0, theirs, 0.0))
+            b_own[j] = past + jnp.where(side == 0, theirs, 0.0)
+
+        @pl.when(t < half)
+        def _():
+            mine = local_forward(own_first + t)
+            theirs = local_forward(other_first + t)
+            w_all[own_first + t], inner_all[own_first + t] = mine
+            w_all[other_first + t], inner_all[other_first + t] = theirs
+
+        @pl.when((t >= 2) & (t < half + 2))
+        def _():
+            c = t - 2
+            mine = local_backward(own_first + c)
+            theirs = local_backward(other_first + c)
+            keep_local_backward(own_first + c, mine)
+            keep_local_backward(other_first + c, theirs)
 
         @pl.when((j >= 1) & (j < half + 1))
         def _():
             c = j - 1
-            parts = backward_local(other_first + c)
             bg(c).wait_recv()
-            backward_later(other_first + c, parts, b_take[c])
+            mine = backward(own_first + c, b_own[c])
+            theirs = backward(other_first + c, b_take[c])
+            keep_backward(own_first + c, mine)
+            keep_backward(other_first + c, theirs)
 
         for s in range(stages + 1):
 
@@ -373,10 +423,15 @@
                     gain_move(s).start()
                 else:
                     gg_ref[...] = gain_sum[s] / scale
+                    stores[4].start()
+                if s < 2:
+                    stores[s].start()
 
         return carry
 
     lax.fori_loop(0, steps, step, 0)
+    stores[2].start()
+    stores[3].start()
 
     def finish(c, carry):
         fx(c).wait_send()
@@ -397,6 +452,19 @@
     lax.fori_loop(0, half, finish, 0)
     for s in range(stages):
         gain_move(s).wait_send()
+    for store in stores:
+        store.wait()
+
+
+def flush(*refs):
+    done = refs[-1]
+    copies = [
+        pltpu.make_async_copy(refs[i], refs[5 + i], done.at[i]) for i in range(5)
+    ]
+    for copy in copies:
+        copy.start()
+    for copy in copies:
+        copy.wait()
 
 
 def fused(queries, keys, values, out_grad, gain):
@@ -417,27 +485,44 @@
     flat = [a.reshape(rows, width) for a in (queries, keys, values, out_grad)]
     state = pltpu.VMEM((half, HEAD, HEAD), F32)
     held = pltpu.VMEM((heads, HEAD, HEAD), BF16)
-    vmem = pl.BlockSpec(memory_space=pltpu.VMEM)
+    wide = pltpu.VMEM((heads, HEAD, HEAD), F32)
+    block = pltpu.VMEM((rows, width), BF16)
+    anywhere = pl.BlockSpec(memory_space=pl.ANY)
     result = pl.pallas_call(
         functools.partial(kernel, count // 2, tuple(hops), scale),
         out_shape=[jax.ShapeDtypeStruct((rows, width), BF16)] * 4
         + [jax.ShapeDtypeStruct((heads, HEAD), F32)],
-        in_specs=[vmem] * 5,
-        out_specs=[vmem] * 5,
+        in_specs=[anywhere] * 5,
+        out_specs=[anywhere] * 5,
         scratch_shapes=[state] * 14
         + [held] * 4
+        + [wide] * 3
         + [
             pltpu.VMEM((stages + 1, heads, HEAD), F32),
             pltpu.VMEM((stages, heads, HEAD), F32),
+            block, block, block, block,
+            pltpu.VMEM((heads, HEAD), F32),
+            block, block, block, block,
+            pltpu.VMEM((heads, HEAD), F32),
             pltpu.SemaphoreType.DMA((6, half)),
             pltpu.SemaphoreType.DMA((6, half)),
             pltpu.SemaphoreType.DMA((stages,)),
             pltpu.SemaphoreType.DMA((stages,)),
+            pltpu.SemaphoreType.DMA((5,)),
+            pltpu.SemaphoreType.DMA((5,)),
         ],
         compiler_params=pltpu.CompilerParams(
-            collective_id=0, has_side_effects=True, vmem_limit_bytes=40 * 1024 * 1024
+            collective_id=0, has_side_effects=True, vmem_limit_bytes=VMEM_LIMIT
         ),
     )(*flat, gain.reshape(heads, HEAD))
+    result = pl.pallas_call(
+        flush,
+        out_shape=[jax.ShapeDtypeStruct(a.shape, a.dtype) for a in result],
+        in_specs=[anywhere] * 5,
+        out_specs=[anywhere] * 5,
+        scratch_shapes=[pltpu.SemaphoreType.DMA((5,))],
+        compiler_params=pltpu.CompilerParams(vmem_limit_bytes=VMEM_LIMIT),
+    )(*result)
     return tuple(a.reshape(shape) for a in result[:4]) + (result[4].reshape(width),)
 
 

time: 84.1 us -> 142 us (1.69)
  Pallas kernels: 74.4 us -> 141 us
  local copies, waits for them, and re-layouts: 8.63 us -> 0 us
    pallas_call x0 -> x1, Pallas kernels: none -> 64.9 us  [fused(): pl.pallas_call(flush, out_shape=[jax.ShapeDtypeStruct(a.shape, a.dtype) f...]
    unnamed x15 -> x0, local copies, waits for them, and re-layouts: 8.63 us -> none
    pallas_call x1, Pallas kernels: 74.4 us -> 76.3 us  [fused(): pl.pallas_call(functools.partial(kernel, count // 2, tuple(hops), scale),...]
where the time goes in v2:
time: 142 us
  Pallas kernels  141 us (99%)
    pallas_call x1, Pallas kernels, fused(): pl.pallas_call(functools.partial(kernel, count // 2, tuple(hops), scale),...  76.3 us
    pallas_call x1, Pallas kernels, fused(): pl.pallas_call(flush, out_shape=[jax.ShapeDtypeStruct(a.shape, a.dtype) f...  64.9 us

profile of v2, /device:TPU:0, one launch (start us, length us, event | category | flops | bytes accessed | tf_op | source)
XLA Modules:
  0.0 141.9 jit_solution(14046188472307176188)
XLA Ops:
  0.6 76.3 %shard_map.92 = (bf16[128,2048]{1,0:T(8,128)(2,1)}, bf16[128,2048]{1,0:T(8,128)(2,1)}, bf16[128,2048]{1,0:T(8,128)(2,1)}, bf16[128,2048]{1,0:T(8,128)(2,1)}, f32[16,128]{1,0:T(8,128)}) custom-call(bf16[128,2048]{1,0:T(8,128)(2,1)} %bitcast.10, bf16[128,2048]{1,0:T(8,128)(2,1)} %bitcast.11, bf16[128,2048]{1,0:T(8,128)(2,1)} %bitcast.12, ...), custom_call_target="tpu_custom_call" | custom-call | tf_op jit(solution)/shard_map/pallas_call | solution.py:491
  76.9 64.9 %shard_map.93 = (bf16[128,2048]{1,0:T(8,128)(2,1)}, bf16[128,2048]{1,0:T(8,128)(2,1)}, bf16[128,2048]{1,0:T(8,128)(2,1)}, bf16[128,2048]{1,0:T(8,128)(2,1)}, f32[16,128]{1,0:T(8,128)}) custom-call(bf16[128,2048]{1,0:T(8,128)(2,1)} %get-tuple-element.15.refs_0_, bf16[128,2048]{1,0:T(8,128)(2,1)} %get-tuple-element.16.refs_1_, ...), custom_call_target="tpu_custom_call" | custom-call | tf_op jit(solution)/shard_map/pallas_call | solution.py:518

commit v3 on v2

--- a/solution.py
+++ b/solution.py
@@ -12,6 +12,7 @@
 GROUP = 128
 LAG_FIRST = 2
 LAG_HOP = 2
+AHEAD = 2
 VMEM_LIMIT = 56 * 1024 * 1024
 MESH = pl.DeviceIdType.MESH
 F32 = jnp.float32
@@ -170,6 +171,13 @@
     partner = {"seq": flip(place, 1)}
     before = {"seq": place - 2}
     after = {"seq": place + 2}
+    def needed(sender, at_end):
+        return jnp.logical_not((side == sender) & jnp.logical_not(at_end))
+
+    fx_send, fx_wait = needed(1, has_after), needed(0, has_after)
+    fg_send, fg_wait = needed(1, has_before), needed(0, has_before)
+    bx_send, bx_wait = needed(0, has_before), needed(1, has_before)
+    bg_send, bg_wait = needed(0, has_after), needed(1, has_after)
     own_first = side * half
     other_first = (1 - side) * half
 
@@ -310,23 +318,42 @@
     def keep_backward(h, results):
         dk_ref[:, cols(h)], dv_ref[:, cols(h)] = results
 
-    @pl.when(jnp.logical_not(has_before))
-    def _():
-        fz_in[...] = jnp.zeros_like(fz_in)
-
-    @pl.when(jnp.logical_not(has_after))
-    def _():
-        bz_in[...] = jnp.zeros_like(bz_in)
+    def clear(ref, condition):
+        @pl.when(condition)
+        def _():
+            ref[...] = jnp.zeros_like(ref)
+
+    clear(fz_in, jnp.logical_not(has_before))
+    clear(bz_in, jnp.logical_not(has_after))
+    clear(f_take, jnp.logical_not(fg_wait))
+    clear(b_take, jnp.logical_not(bg_wait))
 
     loads[0].wait()
     loads[1].wait()
     f_src[0] = key_value(other_first)
     ends = has_before.astype(jnp.int32) + has_after.astype(jnp.int32)
     pl.semaphore_wait(barrier, len(peers) + ends)
-    fx(0).start()
+
+    def start_if(condition, copy):
+        @pl.when(condition)
+        def _():
+            copy.start()
+
+    def recv_if(condition, copy):
+        @pl.when(condition)
+        def _():
+            copy.wait_recv()
+
+    def sent_if(condition, copy):
+        @pl.when(condition)
+        def _():
+            copy.wait_send()
+
+    start_if(fx_send, fx(0))
     for c in range(1, half):
         f_src[c] = key_value(other_first + c)
-        fx(c).start()
+        if c < AHEAD:
+            start_if(fx_send, fx(c))
     for c in range(half):
         f_own[c] = key_value(own_first + c)
     for load in loads[2:]:
@@ -338,31 +365,25 @@
     def step(t, carry):
         @pl.when(t < half)
         def _():
-            fx(t).wait_recv()
-
-            @pl.when(has_before)
-            def _():
-                fz(t, partner).wait_recv()
+            recv_if(fx_wait, fx(t))
+            recv_if(has_before, fz(t, partner))
 
             past, mine, theirs = fz_in[t], f_own[t], f_in[t]
             fz_out[t] = past + (mine + theirs)
-
-            @pl.when(has_after)
-            def _():
-                fz(t, after).start()
-
+            start_if(has_after, fz(t, after))
             f_give[t] = past + jnp.where(side == 0, mine, 0.0)
-            fg(t).start()
+            start_if(fg_send, fg(t))
+            start_if(fx_send & (t < half - AHEAD), fx(jnp.minimum(t + AHEAD, half - 1)))
             f_own[t] = past + jnp.where(side == 1, theirs, 0.0)
 
         @pl.when((t >= 1) & (t < half + 1))
         def _():
             c = t - 1
-            fg(c).wait_recv()
+            recv_if(fg_wait, fg(c))
             theirs = forward(other_first + c, f_take[c])
             mine = forward(own_first + c, f_own[c])
             b_src[c] = theirs[0]
-            bx(c).start()
+            start_if(bx_send, bx(c))
             b_own[c] = mine[0]
             keep_forward(other_first + c, theirs)
             keep_forward(own_first + c, mine)
@@ -371,21 +392,14 @@
 
         @pl.when((j >= 0) & (j < half))
         def _():
-            bx(j).wait_recv()
-
-            @pl.when(has_after)
-            def _():
-                bz(j, partner).wait_recv()
+            recv_if(bx_wait, bx(j))
+            recv_if(has_after, bz(j, partner))
 
             past, mine, theirs = bz_in[j], b_own[j], b_in[j]
             bz_out[j] = past + (mine + theirs)
-
-            @pl.when(has_before)
-            def _():
-                bz(j, before).start()
-
+            start_if(has_before, bz(j, before))
             b_give[j] = past + jnp.where(side == 1, mine, 0.0)
-            bg(j).start()
+            start_if(bg_send, bg(j))
             b_own[j] = past + jnp.where(side == 0, theirs, 0.0)
 
         @pl.when(t < half)
@@ -406,7 +420,7 @@
         @pl.when((j >= 1) & (j < half + 1))
         def _():
             c = j - 1
-            bg(c).wait_recv()
+            recv_if(bg_wait, bg(c))
             mine = backward(own_first + c, b_own[c])
             theirs = backward(other_first + c, b_take[c])
             keep_backward(own_first + c, mine)
@@ -434,19 +448,12 @@
     stores[3].start()
 
     def finish(c, carry):
-        fx(c).wait_send()
-        fg(c).wait_send()
-        bx(c).wait_send()
-        bg(c).wait_send()
-
-        @pl.when(has_after)
-        def _():
-            fz(c, after).wait_send()
-
-        @pl.when(has_before)
-        def _():
-            bz(c, before).wait_send()
-
+        sent_if(fx_send, fx(c))
+        sent_if(fg_send, fg(c))
+        sent_if(bx_send, bx(c))
+        sent_if(bg_send, bg(c))
+        sent_if(has_after, fz(c, after))
+        sent_if(has_before, bz(c, before))
         return carry
 
     lax.fori_loop(0, half, finish, 0)
@@ -457,14 +464,17 @@
 
 
 def flush(*refs):
-    done = refs[-1]
-    copies = [
-        pltpu.make_async_copy(refs[i], refs[5 + i], done.at[i]) for i in range(5)
-    ]
-    for copy in copies:
-        copy.start()
-    for copy in copies:
-        copy.wait()
+    source, target, held = refs[:5], refs[5:10], refs[10:15]
+    sems = refs[15]
+    reads = [pltpu.make_async_copy(source[i], held[i], sems.at[0, i]) for i in range(5)]
+    writes = [pltpu.make_async_copy(held[i], target[i], sems.at[1, i]) for i in range(5)]
+    for read in reads:
+        read.start()
+    for read, write in zip(reads, writes):
+        read.wait()
+        write.start()
+    for write in writes:
+        write.wait()
 
 
 def fused(queries, keys, values, out_grad, gain):
@@ -520,7 +530,8 @@
         out_shape=[jax.ShapeDtypeStruct(a.shape, a.dtype) for a in result],
         in_specs=[anywhere] * 5,
         out_specs=[anywhere] * 5,
-        scratch_shapes=[pltpu.SemaphoreType.DMA((5,))],
+        scratch_shapes=[pltpu.VMEM(a.shape, a.dtype) for a in result]
+        + [pltpu.SemaphoreType.DMA((2, 5))],
         compiler_params=pltpu.CompilerParams(vmem_limit_bytes=VMEM_LIMIT),
     )(*result)
     return tuple(a.reshape(shape) for a in result[:4]) + (result[4].reshape(width),)

time: 142 us -> 76.1 us (0.54)
  Pallas kernels: 141 us -> 75.3 us
    pallas_call x1, Pallas kernels: 64.9 us -> 2.44 us  [fused(): pl.pallas_call(flush, out_shape=[jax.ShapeDtypeStruct(a.shape, a.dtype) f...]
    pallas_call x1, Pallas kernels: 76.3 us -> 72.9 us  [fused(): pl.pallas_call(functools.partial(kernel, count // 2, tuple(hops), scale),...]
where the time goes in v3:
time: 76.1 us; the launch traced here: 75.9 us
  Pallas kernels  75.3 us (99%)
    pallas_call x1, Pallas kernels, fused(): pl.pallas_call(functools.partial(kernel, count // 2, tuple(hops), scale),...  72.9 us
    pallas_call x1, Pallas kernels, fused(): pl.pallas_call(flush, out_shape=[jax.ShapeDtypeStruct(a.shape, a.dtype) f...  2.44 us

profile of v3, /device:TPU:0, one launch (start us, length us, event | category | flops | bytes accessed | tf_op | source)
XLA Modules:
  0.0 75.9 jit_solution(8636211348941709196)
XLA Ops:
  0.6 72.9 %shard_map.92 = (bf16[128,2048]{1,0:T(8,128)(2,1)}, bf16[128,2048]{1,0:T(8,128)(2,1)}, bf16[128,2048]{1,0:T(8,128)(2,1)}, bf16[128,2048]{1,0:T(8,128)(2,1)}, f32[16,128]{1,0:T(8,128)}) custom-call(bf16[128,2048]{1,0:T(8,128)(2,1)} %bitcast.10, bf16[128,2048]{1,0:T(8,128)(2,1)} %bitcast.11, bf16[128,2048]{1,0:T(8,128)(2,1)} %bitcast.12, ...), custom_call_target="tpu_custom_call" | custom-call | tf_op jit(solution)/shard_map/pallas_call | solution.py:501
  73.5 2.4 %shard_map.93 = (bf16[128,2048]{1,0:T(8,128)(2,1)}, bf16[128,2048]{1,0:T(8,128)(2,1)}, bf16[128,2048]{1,0:T(8,128)(2,1)}, bf16[128,2048]{1,0:T(8,128)(2,1)}, f32[16,128]{1,0:T(8,128)}) custom-call(bf16[128,2048]{1,0:T(8,128)(2,1)} %get-tuple-element.15.refs_0_, bf16[128,2048]{1,0:T(8,128)(2,1)} %get-tuple-element.16.refs_1_, ...), custom_call_target="tpu_custom_call" | custom-call | tf_op jit(solution)/shard_map/pallas_call | solution.py:528

commit v4 on v3

--- a/solution.py
+++ b/solution.py
@@ -360,7 +360,21 @@
         load.wait()
 
     lag = LAG_FIRST + LAG_HOP * (pairs - 1 - pair)
-    steps = max(half + 1 + LAG_FIRST + LAG_HOP * (pairs - 1), half + stages + 1)
+    late = 2 * pair >= pairs
+    local_lag = jnp.where(late, half + 1, 2)
+    final_lag = jnp.maximum(lag + 1, half + 2)
+    most = max(LAG_FIRST + LAG_HOP * (pairs - 1) + 1, half + 2)
+    steps = half + max(most, stages + 1)
+
+    def local_step(c):
+        mine = local_forward(own_first + c)
+        theirs = local_forward(other_first + c)
+        w_all[own_first + c], inner_all[own_first + c] = mine
+        w_all[other_first + c], inner_all[other_first + c] = theirs
+
+    @pl.when(late)
+    def _():
+        lax.fori_loop(0, half, lambda c, carry: (local_step(c), carry)[1], 0)
 
     def step(t, carry):
         @pl.when(t < half)
@@ -402,29 +416,28 @@
             start_if(bg_send, bg(j))
             b_own[j] = past + jnp.where(side == 0, theirs, 0.0)
 
-        @pl.when(t < half)
-        def _():
-            mine = local_forward(own_first + t)
-            theirs = local_forward(other_first + t)
-            w_all[own_first + t], inner_all[own_first + t] = mine
-            w_all[other_first + t], inner_all[other_first + t] = theirs
-
-        @pl.when((t >= 2) & (t < half + 2))
-        def _():
-            c = t - 2
-            mine = local_backward(own_first + c)
-            theirs = local_backward(other_first + c)
-            keep_local_backward(own_first + c, mine)
-            keep_local_backward(other_first + c, theirs)
-
-        @pl.when((j >= 1) & (j < half + 1))
-        def _():
-            c = j - 1
-            recv_if(bg_wait, bg(c))
-            mine = backward(own_first + c, b_own[c])
-            theirs = backward(other_first + c, b_take[c])
-            keep_backward(own_first + c, mine)
-            keep_backward(other_first + c, theirs)
+        @pl.when((t < half) & jnp.logical_not(late))
+        def _():
+            local_step(t)
+
+        b = t - local_lag
+
+        @pl.when((b >= 0) & (b < half))
+        def _():
+            mine = local_backward(own_first + b)
+            theirs = local_backward(other_first + b)
+            keep_local_backward(own_first + b, mine)
+            keep_local_backward(other_first + b, theirs)
+
+        e = t - final_lag
+
+        @pl.when((e >= 0) & (e < half))
+        def _():
+            recv_if(bg_wait, bg(e))
+            mine = backward(own_first + e, b_own[e])
+            theirs = backward(other_first + e, b_take[e])
+            keep_backward(own_first + e, mine)
+            keep_backward(other_first + e, theirs)
 
         for s in range(stages + 1):
 
@@ -438,14 +451,14 @@
                 else:
                     gg_ref[...] = gain_sum[s] / scale
                     stores[4].start()
-                if s < 2:
-                    stores[s].start()
+                if s == 0:
+                    stores[0].start()
 
         return carry
 
     lax.fori_loop(0, steps, step, 0)
-    stores[2].start()
-    stores[3].start()
+    for store in stores[1:4]:
+        store.start()
 
     def finish(c, carry):
         sent_if(fx_send, fx(c))

time: 76.1 us -> 74.4 us (0.978)
  Pallas kernels: 75.3 us -> 73.6 us
    pallas_call x1, Pallas kernels: 72.9 us -> 71.1 us  [fused(): pl.pallas_call(functools.partial(kernel, count // 2, tuple(hops), scale),...]
where the time goes in v4:
time: 74.4 us; the launch traced here: 74.2 us
  Pallas kernels  73.6 us (99%)
    pallas_call x1, Pallas kernels, fused(): pl.pallas_call(functools.partial(kernel, count // 2, tuple(hops), scale),...  71.1 us
    pallas_call x1, Pallas kernels, fused(): pl.pallas_call(flush, out_shape=[jax.ShapeDtypeStruct(a.shape, a.dtype) f...  2.44 us

profile of v4, /device:TPU:0, one launch (start us, length us, event | category | flops | bytes accessed | tf_op | source)
XLA Modules:
  0.0 74.2 jit_solution(15675646735824305243)
XLA Ops:
  0.6 71.1 %shard_map.92 = (bf16[128,2048]{1,0:T(8,128)(2,1)}, bf16[128,2048]{1,0:T(8,128)(2,1)}, bf16[128,2048]{1,0:T(8,128)(2,1)}, bf16[128,2048]{1,0:T(8,128)(2,1)}, f32[16,128]{1,0:T(8,128)}) custom-call(bf16[128,2048]{1,0:T(8,128)(2,1)} %bitcast.10, bf16[128,2048]{1,0:T(8,128)(2,1)} %bitcast.11, bf16[128,2048]{1,0:T(8,128)(2,1)} %bitcast.12, ...), custom_call_target="tpu_custom_call" | custom-call | tf_op jit(solution)/shard_map/pallas_call | solution.py:514
  71.8 2.4 %shard_map.93 = (bf16[128,2048]{1,0:T(8,128)(2,1)}, bf16[128,2048]{1,0:T(8,128)(2,1)}, bf16[128,2048]{1,0:T(8,128)(2,1)}, bf16[128,2048]{1,0:T(8,128)(2,1)}, f32[16,128]{1,0:T(8,128)}) custom-call(bf16[128,2048]{1,0:T(8,128)(2,1)} %get-tuple-element.15.refs_0_, bf16[128,2048]{1,0:T(8,128)(2,1)} %get-tuple-element.16.refs_1_, ...), custom_call_target="tpu_custom_call" | custom-call | tf_op jit(solution)/shard_map/pallas_call | solution.py:541

commit v5 on v4

--- a/solution.py
+++ b/solution.py
@@ -10,9 +10,11 @@
 
 HEAD = 128
 GROUP = 128
-LAG_FIRST = 2
+FORWARD_LAG = 3
+LAG_FIRST = 5
 LAG_HOP = 2
-AHEAD = 2
+FINAL_LAG = 3
+AHEAD = 4
 VMEM_LIMIT = 56 * 1024 * 1024
 MESH = pl.DeviceIdType.MESH
 F32 = jnp.float32
@@ -361,10 +363,11 @@
 
     lag = LAG_FIRST + LAG_HOP * (pairs - 1 - pair)
     late = 2 * pair >= pairs
-    local_lag = jnp.where(late, half + 1, 2)
-    final_lag = jnp.maximum(lag + 1, half + 2)
-    most = max(LAG_FIRST + LAG_HOP * (pairs - 1) + 1, half + 2)
-    steps = half + max(most, stages + 1)
+    forward_end = half + FORWARD_LAG
+    local_lag = jnp.where(late, forward_end, FORWARD_LAG + 1)
+    final_lag = jnp.maximum(lag + FINAL_LAG, forward_end + 1)
+    most = max(LAG_FIRST + LAG_HOP * (pairs - 1) + FINAL_LAG, forward_end + 1)
+    steps = max(half + most, forward_end + stages)
 
     def local_step(c):
         mine = local_forward(own_first + c)
@@ -390,9 +393,9 @@
             start_if(fx_send & (t < half - AHEAD), fx(jnp.minimum(t + AHEAD, half - 1)))
             f_own[t] = past + jnp.where(side == 1, theirs, 0.0)
 
-        @pl.when((t >= 1) & (t < half + 1))
-        def _():
-            c = t - 1
+        @pl.when((t >= FORWARD_LAG) & (t < half + FORWARD_LAG))
+        def _():
+            c = t - FORWARD_LAG
             recv_if(fg_wait, fg(c))
             theirs = forward(other_first + c, f_take[c])
             mine = forward(own_first + c, f_own[c])
@@ -441,7 +444,7 @@
 
         for s in range(stages + 1):
 
-            @pl.when(t == half + s)
+            @pl.when(t == forward_end - 1 + s)
             def _(s=s):
                 if s > 0:
                     gain_move(s - 1).wait_recv()

time: 74.4 us -> 72.7 us (0.977)
  Pallas kernels: 73.6 us -> 71.9 us
    pallas_call x1, Pallas kernels: 71.1 us -> 69.5 us  [fused(): pl.pallas_call(functools.partial(kernel, count // 2, tuple(hops), scale),...]
where the time goes in v5:
time: 72.7 us; the launch traced here: 72.6 us
  Pallas kernels  71.9 us (99%)
    pallas_call x1, Pallas kernels, fused(): pl.pallas_call(functools.partial(kernel, count // 2, tuple(hops), scale),...  69.5 us
    pallas_call x1, Pallas kernels, fused(): pl.pallas_call(flush, out_shape=[jax.ShapeDtypeStruct(a.shape, a.dtype) f...  2.44 us

profile of v5, /device:TPU:0, one launch (start us, length us, event | category | flops | bytes accessed | tf_op | source)
XLA Modules:
  0.0 72.6 jit_solution(1303018310411378400)
XLA Ops:
  0.6 69.5 %shard_map.92 = (bf16[128,2048]{1,0:T(8,128)(2,1)}, bf16[128,2048]{1,0:T(8,128)(2,1)}, bf16[128,2048]{1,0:T(8,128)(2,1)}, bf16[128,2048]{1,0:T(8,128)(2,1)}, f32[16,128]{1,0:T(8,128)}) custom-call(bf16[128,2048]{1,0:T(8,128)(2,1)} %bitcast.10, bf16[128,2048]{1,0:T(8,128)(2,1)} %bitcast.11, bf16[128,2048]{1,0:T(8,128)(2,1)} %bitcast.12, ...), custom_call_target="tpu_custom_call" | custom-call | tf_op jit(solution)/shard_map/pallas_call | solution.py:517
  70.1 2.4 %shard_map.93 = (bf16[128,2048]{1,0:T(8,128)(2,1)}, bf16[128,2048]{1,0:T(8,128)(2,1)}, bf16[128,2048]{1,0:T(8,128)(2,1)}, bf16[128,2048]{1,0:T(8,128)(2,1)}, f32[16,128]{1,0:T(8,128)}) custom-call(bf16[128,2048]{1,0:T(8,128)(2,1)} %get-tuple-element.15.refs_0_, bf16[128,2048]{1,0:T(8,128)(2,1)} %get-tuple-element.16.refs_1_, ...), custom_call_target="tpu_custom_call" | custom-call | tf_op jit(solution)/shard_map/pallas_call | solution.py:544

commit v6 on v5

--- a/solution.py
+++ b/solution.py
@@ -14,7 +14,8 @@
 LAG_FIRST = 5
 LAG_HOP = 2
 FINAL_LAG = 3
-AHEAD = 4
+AHEAD_FIRST = 2
+AHEAD_HOP = 2
 VMEM_LIMIT = 56 * 1024 * 1024
 MESH = pl.DeviceIdType.MESH
 F32 = jnp.float32
@@ -351,11 +352,11 @@
         def _():
             copy.wait_send()
 
+    ahead = jnp.minimum(half, AHEAD_FIRST + AHEAD_HOP * pair)
     start_if(fx_send, fx(0))
     for c in range(1, half):
         f_src[c] = key_value(other_first + c)
-        if c < AHEAD:
-            start_if(fx_send, fx(c))
+        start_if(fx_send & (c < ahead), fx(c))
     for c in range(half):
         f_own[c] = key_value(own_first + c)
     for load in loads[2:]:
@@ -365,8 +366,9 @@
     late = 2 * pair >= pairs
     forward_end = half + FORWARD_LAG
     local_lag = jnp.where(late, forward_end, FORWARD_LAG + 1)
-    final_lag = jnp.maximum(lag + FINAL_LAG, forward_end + 1)
-    most = max(LAG_FIRST + LAG_HOP * (pairs - 1) + FINAL_LAG, forward_end + 1)
+    give_lag = jnp.maximum(lag, forward_end)
+    final_lag = give_lag + FINAL_LAG
+    most = max(LAG_FIRST + LAG_HOP * (pairs - 1), forward_end) + FINAL_LAG
     steps = max(half + most, forward_end + stages)
 
     def local_step(c):
@@ -390,7 +392,7 @@
             start_if(has_after, fz(t, after))
             f_give[t] = past + jnp.where(side == 0, mine, 0.0)
             start_if(fg_send, fg(t))
-            start_if(fx_send & (t < half - AHEAD), fx(jnp.minimum(t + AHEAD, half - 1)))
+            start_if(fx_send & (t < half - ahead), fx(jnp.minimum(t + ahead, half - 1)))
             f_own[t] = past + jnp.where(side == 1, theirs, 0.0)
 
         @pl.when((t >= FORWARD_LAG) & (t < half + FORWARD_LAG))
@@ -416,8 +418,13 @@
             bz_out[j] = past + (mine + theirs)
             start_if(has_before, bz(j, before))
             b_give[j] = past + jnp.where(side == 1, mine, 0.0)
-            start_if(bg_send, bg(j))
             b_own[j] = past + jnp.where(side == 0, theirs, 0.0)
+
+        u = t - give_lag
+
+        @pl.when((u >= 0) & (u < half))
+        def _():
+            start_if(bg_send, bg(u))
 
         @pl.when((t < half) & jnp.logical_not(late))
         def _():

time: 72.7 us -> 69 us (0.949)
  Pallas kernels: 71.9 us -> 68.2 us
    pallas_call x1, Pallas kernels: 69.5 us -> 65.7 us  [fused(): pl.pallas_call(functools.partial(kernel, count // 2, tuple(hops), scale),...]
where the time goes in v6:
time: 69 us; the launch traced here: 68.8 us
  Pallas kernels  68.2 us (99%)
    pallas_call x1, Pallas kernels, fused(): pl.pallas_call(functools.partial(kernel, count // 2, tuple(hops), scale),...  65.7 us
    pallas_call x1, Pallas kernels, fused(): pl.pallas_call(flush, out_shape=[jax.ShapeDtypeStruct(a.shape, a.dtype) f...  2.44 us

profile of v6, /device:TPU:0, one launch (start us, length us, event | category | flops | bytes accessed | tf_op | source)
XLA Modules:
  0.0 68.8 jit_solution(8917269095530478188)
XLA Ops:
  0.6 65.7 %shard_map.92 = (bf16[128,2048]{1,0:T(8,128)(2,1)}, bf16[128,2048]{1,0:T(8,128)(2,1)}, bf16[128,2048]{1,0:T(8,128)(2,1)}, bf16[128,2048]{1,0:T(8,128)(2,1)}, f32[16,128]{1,0:T(8,128)}) custom-call(bf16[128,2048]{1,0:T(8,128)(2,1)} %bitcast.10, bf16[128,2048]{1,0:T(8,128)(2,1)} %bitcast.11, bf16[128,2048]{1,0:T(8,128)(2,1)} %bitcast.12, ...), custom_call_target="tpu_custom_call" | custom-call | tf_op jit(solution)/shard_map/pallas_call | solution.py:524
  66.4 2.4 %shard_map.93 = (bf16[128,2048]{1,0:T(8,128)(2,1)}, bf16[128,2048]{1,0:T(8,128)(2,1)}, bf16[128,2048]{1,0:T(8,128)(2,1)}, bf16[128,2048]{1,0:T(8,128)(2,1)}, f32[16,128]{1,0:T(8,128)}) custom-call(bf16[128,2048]{1,0:T(8,128)(2,1)} %get-tuple-element.15.refs_0_, bf16[128,2048]{1,0:T(8,128)(2,1)} %get-tuple-element.16.refs_1_, ...), custom_call_target="tpu_custom_call" | custom-call | tf_op jit(solution)/shard_map/pallas_call | solution.py:551

commit v7 on v6

--- a/solution.py
+++ b/solution.py
@@ -10,6 +10,7 @@
 
 HEAD = 128
 GROUP = 128
+PARTS = 2
 FORWARD_LAG = 3
 LAG_FIRST = 5
 LAG_HOP = 2
@@ -162,7 +163,7 @@
     w_all, hi_all, lo_all, go_all, inner_all, dk_all, dv_all, gain_sum, gain_in,
     q_ref, k_ref, v_ref, g_ref, gain_ref,
     out_ref, dq_ref, dk_ref, dv_ref, gg_ref,
-    send, recv, gain_send, gain_recv, load_sem, store_sem,
+    send, recv, chain_send, chain_recv, gain_send, gain_recv, load_sem, store_sem,
 ):
     half = f_own.shape[0]
     stages = len(hops)
@@ -230,20 +231,30 @@
     def fx(c):
         return move(0, f_src, f_in, c, partner)
 
-    def fz(c, device):
-        return move(1, fz_out, fz_in, c, device)
+    def chain_rows(p):
+        return pl.ds(p * (HEAD // PARTS), HEAD // PARTS)
+
+    def chain_move(kind, src, dst, c, p, device):
+        return pltpu.make_async_remote_copy(
+            src_ref=src.at[c, chain_rows(p)], dst_ref=dst.at[c, chain_rows(p)],
+            send_sem=chain_send.at[kind, c, p], recv_sem=chain_recv.at[kind, c, p],
+            device_id=device, device_id_type=MESH,
+        )
+
+    def fz(c, p, device):
+        return chain_move(0, fz_out, fz_in, c, p, device)
 
     def fg(c):
-        return move(2, f_give, f_take, c, partner)
+        return move(1, f_give, f_take, c, partner)
 
     def bx(c):
-        return move(3, b_src, b_in, c, partner)
-
-    def bz(c, device):
-        return move(4, bz_out, bz_in, c, device)
+        return move(2, b_src, b_in, c, partner)
+
+    def bz(c, p, device):
+        return chain_move(1, bz_out, bz_in, c, p, device)
 
     def bg(c):
-        return move(5, b_give, b_take, c, partner)
+        return move(3, b_give, b_take, c, partner)
 
     def gain_move(s):
         axis, bit = hops[s]
@@ -385,11 +396,12 @@
         @pl.when(t < half)
         def _():
             recv_if(fx_wait, fx(t))
-            recv_if(has_before, fz(t, partner))
-
+            for p in range(PARTS):
+                rows = chain_rows(p)
+                recv_if(has_before, fz(t, p, partner))
+                fz_out[t, rows] = fz_in[t, rows] + (f_own[t, rows] + f_in[t, rows])
+                start_if(has_after, fz(t, p, after))
             past, mine, theirs = fz_in[t], f_own[t], f_in[t]
-            fz_out[t] = past + (mine + theirs)
-            start_if(has_after, fz(t, after))
             f_give[t] = past + jnp.where(side == 0, mine, 0.0)
             start_if(fg_send, fg(t))
             start_if(fx_send & (t < half - ahead), fx(jnp.minimum(t + ahead, half - 1)))
@@ -412,11 +424,12 @@
         @pl.when((j >= 0) & (j < half))
         def _():
             recv_if(bx_wait, bx(j))
-            recv_if(has_after, bz(j, partner))
-
+            for p in range(PARTS):
+                rows = chain_rows(p)
+                recv_if(has_after, bz(j, p, partner))
+                bz_out[j, rows] = bz_in[j, rows] + (b_own[j, rows] + b_in[j, rows])
+                start_if(has_before, bz(j, p, before))
             past, mine, theirs = bz_in[j], b_own[j], b_in[j]
-            bz_out[j] = past + (mine + theirs)
-            start_if(has_before, bz(j, before))
             b_give[j] = past + jnp.where(side == 1, mine, 0.0)
             b_own[j] = past + jnp.where(side == 0, theirs, 0.0)
 
@@ -438,6 +451,10 @@
             theirs = local_backward(other_first + b)
             keep_local_backward(own_first + b, mine)
             keep_local_backward(other_first + b, theirs)
+
+            @pl.when(b == half - 1)
+            def _():
+                stores[1].start()
 
         e = t - final_lag
 
@@ -467,7 +484,7 @@
         return carry
 
     lax.fori_loop(0, steps, step, 0)
-    for store in stores[1:4]:
+    for store in stores[2:4]:
         store.start()
 
     def finish(c, carry):
@@ -475,8 +492,9 @@
         sent_if(fg_send, fg(c))
         sent_if(bx_send, bx(c))
         sent_if(bg_send, bg(c))
-        sent_if(has_after, fz(c, after))
-        sent_if(has_before, bz(c, before))
+        for p in range(PARTS):
+            sent_if(has_after, fz(c, p, after))
+            sent_if(has_before, bz(c, p, before))
         return carry
 
     lax.fori_loop(0, half, finish, 0)
@@ -537,8 +555,10 @@
             pltpu.VMEM((heads, HEAD), F32),
             block, block, block, block,
             pltpu.VMEM((heads, HEAD), F32),
-            pltpu.SemaphoreType.DMA((6, half)),
-            pltpu.SemaphoreType.DMA((6, half)),
+            pltpu.SemaphoreType.DMA((4, half)),
+            pltpu.SemaphoreType.DMA((4, half)),
+            pltpu.SemaphoreType.DMA((2, half, PARTS)),
+            pltpu.SemaphoreType.DMA((2, half, PARTS)),
             pltpu.SemaphoreType.DMA((stages,)),
             pltpu.SemaphoreType.DMA((stages,)),
             pltpu.SemaphoreType.DMA((5,)),

time: 69 us -> 68.3 us (0.990)
  Pallas kernels: 68.2 us -> 67.5 us
where the time goes in v7:
time: 68.3 us; the launch traced here: 68.2 us
  Pallas kernels  67.5 us (99%)
    pallas_call x1, Pallas kernels, fused(): pl.pallas_call(functools.partial(kernel, count // 2, tuple(hops), scale),...  65.1 us
    pallas_call x1, Pallas kernels, fused(): pl.pallas_call(flush, out_shape=[jax.ShapeDtypeStruct(a.shape, a.dtype) f...  2.44 us

profile of v7, /device:TPU:0, one launch (start us, length us, event | category | flops | bytes accessed | tf_op | source)
XLA Modules:
  0.0 68.2 jit_solution(13003097827816323318)
XLA Ops:
  0.6 65.1 %shard_map.92 = (bf16[128,2048]{1,0:T(8,128)(2,1)}, bf16[128,2048]{1,0:T(8,128)(2,1)}, bf16[128,2048]{1,0:T(8,128)(2,1)}, bf16[128,2048]{1,0:T(8,128)(2,1)}, f32[16,128]{1,0:T(8,128)}) custom-call(bf16[128,2048]{1,0:T(8,128)(2,1)} %bitcast.10, bf16[128,2048]{1,0:T(8,128)(2,1)} %bitcast.11, bf16[128,2048]{1,0:T(8,128)(2,1)} %bitcast.12, ...), custom_call_target="tpu_custom_call" | custom-call | tf_op jit(solution)/shard_map/pallas_call | solution.py:542
  65.7 2.4 %shard_map.93 = (bf16[128,2048]{1,0:T(8,128)(2,1)}, bf16[128,2048]{1,0:T(8,128)(2,1)}, bf16[128,2048]{1,0:T(8,128)(2,1)}, bf16[128,2048]{1,0:T(8,128)(2,1)}, f32[16,128]{1,0:T(8,128)}) custom-call(bf16[128,2048]{1,0:T(8,128)(2,1)} %get-tuple-element.15.refs_0_, bf16[128,2048]{1,0:T(8,128)(2,1)} %get-tuple-element.16.refs_1_, ...), custom_call_target="tpu_custom_call" | custom-call | tf_op jit(solution)/shard_map/pallas_call | solution.py:571

commit v8 on v7

--- a/solution.py
+++ b/solution.py
@@ -191,7 +191,7 @@
             (k_hbm, k_ref), (v_hbm, v_ref), (q_hbm, q_ref), (g_hbm, g_ref), (gain_hbm, gain_ref),
         ))
     ]
-    for load in loads:
+    for load in loads[:2]:
         load.start()
 
     stores = [
@@ -342,8 +342,10 @@
     clear(f_take, jnp.logical_not(fg_wait))
     clear(b_take, jnp.logical_not(bg_wait))
 
-    loads[0].wait()
-    loads[1].wait()
+    for load in loads[:2]:
+        load.wait()
+    for load in loads[2:]:
+        load.start()
     f_src[0] = key_value(other_first)
     ends = has_before.astype(jnp.int32) + has_after.astype(jnp.int32)
     pl.semaphore_wait(barrier, len(peers) + ends)
@@ -377,7 +379,7 @@
     late = 2 * pair >= pairs
     forward_end = half + FORWARD_LAG
     local_lag = jnp.where(late, forward_end, FORWARD_LAG + 1)
-    give_lag = jnp.maximum(lag, forward_end)
+    give_lag = jnp.maximum(lag, forward_end - 1)
     final_lag = give_lag + FINAL_LAG
     most = max(LAG_FIRST + LAG_HOP * (pairs - 1), forward_end) + FINAL_LAG
     steps = max(half + most, forward_end + stages)
@@ -420,6 +422,11 @@
             keep_forward(own_first + c, mine)
 
         j = t - lag
+        u = t - give_lag
+
+        @pl.when((u >= 0) & (u < half) & (u < j))
+        def _():
+            start_if(bg_send, bg(u))
 
         @pl.when((j >= 0) & (j < half))
         def _():
@@ -433,9 +440,7 @@
             b_give[j] = past + jnp.where(side == 1, mine, 0.0)
             b_own[j] = past + jnp.where(side == 0, theirs, 0.0)
 
-        u = t - give_lag
-
-        @pl.when((u >= 0) & (u < half))
+        @pl.when((u >= 0) & (u < half) & (u == j))
         def _():
             start_if(bg_send, bg(u))
 

time: 68.3 us -> 68.6 us (level)
  no operation moved by 1% of the time
where the time goes in v8:
time: 68.6 us; the launch traced here: 68.5 us
  Pallas kernels  67.8 us (99%)
    pallas_call x1, Pallas kernels, fused(): pl.pallas_call(functools.partial(kernel, count // 2, tuple(hops), scale),...  65.4 us
    pallas_call x1, Pallas kernels, fused(): pl.pallas_call(flush, out_shape=[jax.ShapeDtypeStruct(a.shape, a.dtype) f...  2.44 us

profile of v8, /device:TPU:0, one launch (start us, length us, event | category | flops | bytes accessed | tf_op | source)
XLA Modules:
  0.0 68.5 jit_solution(13244313894319902497)
XLA Ops:
  0.6 65.4 %shard_map.92 = (bf16[128,2048]{1,0:T(8,128)(2,1)}, bf16[128,2048]{1,0:T(8,128)(2,1)}, bf16[128,2048]{1,0:T(8,128)(2,1)}, bf16[128,2048]{1,0:T(8,128)(2,1)}, f32[16,128]{1,0:T(8,128)}) custom-call(bf16[128,2048]{1,0:T(8,128)(2,1)} %bitcast.10, bf16[128,2048]{1,0:T(8,128)(2,1)} %bitcast.11, bf16[128,2048]{1,0:T(8,128)(2,1)} %bitcast.12, ...), custom_call_target="tpu_custom_call" | custom-call | tf_op jit(solution)/shard_map/pallas_call | solution.py:547
  66.0 2.4 %shard_map.93 = (bf16[128,2048]{1,0:T(8,128)(2,1)}, bf16[128,2048]{1,0:T(8,128)(2,1)}, bf16[128,2048]{1,0:T(8,128)(2,1)}, bf16[128,2048]{1,0:T(8,128)(2,1)}, f32[16,128]{1,0:T(8,128)}) custom-call(bf16[128,2048]{1,0:T(8,128)(2,1)} %get-tuple-element.15.refs_0_, bf16[128,2048]{1,0:T(8,128)(2,1)} %get-tuple-element.16.refs_1_, ...), custom_call_target="tpu_custom_call" | custom-call | tf_op jit(solution)/shard_map/pallas_call | solution.py:576

commit v9 on v7

--- a/solution.py
+++ b/solution.py
@@ -10,7 +10,7 @@
 
 HEAD = 128
 GROUP = 128
-PARTS = 2
+PARTS = 4
 FORWARD_LAG = 3
 LAG_FIRST = 5
 LAG_HOP = 2

time: 68.3 us -> 68.6 us (level)
  no operation moved by 1% of the time
where the time goes in v9:
time: 68.6 us; the launch traced here: 68.4 us
  Pallas kernels  67.8 us (99%)
    pallas_call x1, Pallas kernels, fused(): pl.pallas_call(functools.partial(kernel, count // 2, tuple(hops), scale),...  65.4 us
    pallas_call x1, Pallas kernels, fused(): pl.pallas_call(flush, out_shape=[jax.ShapeDtypeStruct(a.shape, a.dtype) f...  2.44 us

profile of v9, /device:TPU:0, one launch (start us, length us, event | category | flops | bytes accessed | tf_op | source)
XLA Modules:
  0.0 68.4 jit_solution(14537078375544236565)
XLA Ops:
  0.6 65.4 %shard_map.92 = (bf16[128,2048]{1,0:T(8,128)(2,1)}, bf16[128,2048]{1,0:T(8,128)(2,1)}, bf16[128,2048]{1,0:T(8,128)(2,1)}, bf16[128,2048]{1,0:T(8,128)(2,1)}, f32[16,128]{1,0:T(8,128)}) custom-call(bf16[128,2048]{1,0:T(8,128)(2,1)} %bitcast.10, bf16[128,2048]{1,0:T(8,128)(2,1)} %bitcast.11, bf16[128,2048]{1,0:T(8,128)(2,1)} %bitcast.12, ...), custom_call_target="tpu_custom_call" | custom-call | tf_op jit(solution)/shard_map/pallas_call | solution.py:542
  66.0 2.4 %shard_map.93 = (bf16[128,2048]{1,0:T(8,128)(2,1)}, bf16[128,2048]{1,0:T(8,128)(2,1)}, bf16[128,2048]{1,0:T(8,128)(2,1)}, bf16[128,2048]{1,0:T(8,128)(2,1)}, f32[16,128]{1,0:T(8,128)}) custom-call(bf16[128,2048]{1,0:T(8,128)(2,1)} %get-tuple-element.15.refs_0_, bf16[128,2048]{1,0:T(8,128)(2,1)} %get-tuple-element.16.refs_1_, ...), custom_call_target="tpu_custom_call" | custom-call | tf_op jit(solution)/shard_map/pallas_call | solution.py:571
